TPU v7x, 32 devices: a whole 2x2x4 slice. The times are simulated.
32 devices in a mesh: shot: 2 (over y), sx: 8 (over z, x), sy: 2 (over core).
Axes of the slice: x: 2, y: 2, z: 4, core: 2. Of those that a mesh axis runs over, the one named last changes fastest.
Arguments:
- pressure: float32 [256, 32, 128], P(('shot', 'sx'), 'sy'), parts along dimension 0, may hold values from -6 to 6
- velocity: float32 [3, 256, 32, 128], P(None, ('shot', 'sx'), 'sy'), parts along dimension 1, may hold values from -6 to 6
- courant: float32 [128, 32, 128], P('sx', 'sy'), may hold values from 0.15 to 0.42
- observed: float32 [4096, 2000], P(('shot', 'sx', 'sy')), parts along dimension 0, may hold values from -6 to 6
- rec_owner: int32 [4096, 1], P(('shot', 'sx', 'sy')), parts along dimension 0, may hold values from 0 to 15; in each aligned block of 128 rows (0 to 127, 128 to 255, ...) at most 16 rows name the same one
- rec_cell: int32 [4096], P(('shot', 'sx', 'sy')), parts along dimension 0, may hold values from 0 to 32767
- src_pos: int32 [2], P('shot'), parts along dimension 0, may hold values from 0 to 524287
- wavelet: float32 [20], replicated, may hold values from -4 to 4
Outputs:
- pressure_out: float32 [256, 32, 128], P(('shot', 'sx'), 'sy'), parts along dimension 0
- velocity_out: float32 [3, 256, 32, 128], P(None, ('shot', 'sx'), 'sy'), parts along dimension 1
- trace_xcorr: float32 [3962], P('shot'), parts along dimension 0
There are 2 independent parts, one for each index of `shot`. A program takes and returns all parts, laid end to end along the dimension named above; an argument that names none is the same for every part. Nothing has to cross between parts.
Inputs may be any that keep to these rules, and one draw needn't show every extreme that they name: `rec_owner`: in each device's block of 128 receivers at most 16 have the same owner; in some blocks one owner has exactly 16.
All inputs are finite; a program needn't handle non-finite values.
Results may differ from a plain program's by a relative error of at most 0.00022.
Values sent between devices are 32-bit elements; how exact they have to be, the bound alone decides.
A program may use at most 64 MiB of HBM per device.

v0:
```python
import math

import jax
import jax.numpy as jnp
from jax import lax
from jax.sharding import PartitionSpec as P

c_one = 9.0 / 8.0
c_two = -1.0 / 24.0


def extended(block, sides, width):
    for axis, dim in sides:
        count = lax.axis_size(axis)
        forward = [(i, i + 1) for i in range(count - 1)]
        backward = [(target, source) for source, target in forward]
        low = lax.ppermute(
            lax.slice_in_dim(block, block.shape[dim] - width, None, axis=dim), axis, forward
        )
        high = lax.ppermute(lax.slice_in_dim(block, 0, width, axis=dim), axis, backward)
        block = jnp.concatenate([low, block, high], axis=dim)
    return block


def ahead(padded, axis, count):

    def part(k):
        return lax.slice_in_dim(padded, 2 + k, 2 + k + count, axis=axis)

    return c_one * (part(1) - part(0)) + c_two * (part(2) - part(-1))


def behind(padded, axis, count):

    def part(k):
        return lax.slice_in_dim(padded, 2 + k, 2 + k + count, axis=axis)

    return c_one * (part(0) - part(-1)) + c_two * (part(1) - part(-2))


def correlate(records, rows, nlag):
    steps = records.shape[0]

    def add_step(step, summed):
        line = lax.dynamic_index_in_dim(records, step, 0, keepdims=False)
        window = lax.dynamic_slice_in_dim(rows, step, nlag, 1)
        return summed + jnp.dot(line, window, precision=lax.Precision.HIGHEST)

    return lax.fori_loop(0, steps, add_step, jnp.zeros((nlag,), jnp.float32))


def body(pressure, velocity, courant, observed, rec_owner, rec_cell, src_pos, wavelet):
    cx, cy, cz = pressure.shape
    count_x = lax.axis_size("sx")
    count_y = lax.axis_size("sy")
    subs = count_x * count_y
    r_dev, nt = observed.shape
    steps = wavelet.shape[0]
    nlag = nt - steps + 1
    cap = max(2, 2 * r_dev // subs)
    index_x = lax.axis_index("sx")
    index_y = lax.axis_index("sy")
    full_y = cy * count_y
    source = src_pos[0]
    src_x = source // (full_y * cz) - index_x * cx
    src_y = source // cz % full_y - index_y * cy
    src_z = source % cz
    grid_x = lax.broadcasted_iota(jnp.int32, (cx, cy, cz), 0)
    grid_y = lax.broadcasted_iota(jnp.int32, (cx, cy, cz), 1)
    grid_z = lax.broadcasted_iota(jnp.int32, (cx, cy, cz), 2)
    source_mask = ((grid_x == src_x) & (grid_y == src_y) & (grid_z == src_z)).astype(jnp.float32)
    owner = rec_owner[:, 0]
    onehot = (owner[:, None] == jnp.arange(subs, dtype=jnp.int32)[None, :]).astype(jnp.int32)
    ranks = jnp.sum(jnp.cumsum(onehot, axis=0) * onehot, axis=1) - 1
    slot_pos = owner * cap + ranks
    cell_buf = (
        jnp.full((subs * cap,), -1.0, jnp.float32).at[slot_pos].set(rec_cell.astype(jnp.float32))
    )
    obs_buf = jnp.zeros((subs * cap, nt), jnp.float32).at[slot_pos].set(observed)
    got_rows, got_cells = (
        lax.all_to_all(
            obs_buf.reshape(subs, cap, nt), ("sx", "sy"), split_axis=0, concat_axis=0, tiled=True
        ),
        lax.all_to_all(
            cell_buf.reshape(subs, cap), ("sx", "sy"), split_axis=0, concat_axis=0, tiled=True
        ),
    )
    got_rows = got_rows.reshape(subs * cap, nt)
    got_cells = got_cells.reshape(subs * cap)
    valid = (got_cells >= 0.0).astype(jnp.float32)
    cell_index = jnp.maximum(got_cells, 0.0).astype(jnp.int32)

    def advance(carry, amplitude):
        press, vel_x, vel_y, vel_z = carry
        rim = extended(press, (("sx", 0), ("sy", 1)), 2)
        grad_x = ahead(rim[:, 2 : 2 + cy, :], 0, cx)
        grad_y = ahead(rim[2 : 2 + cx, :, :], 1, cy)
        core = rim[2 : 2 + cx, 2 : 2 + cy, :]
        grad_z = ahead(jnp.pad(core, ((0, 0), (0, 0), (2, 2))), 2, cz)
        vel_x = vel_x - courant * grad_x
        vel_y = vel_y - courant * grad_y
        vel_z = vel_z - courant * grad_z
        rim_x = extended(vel_x, (("sx", 0),), 2)
        rim_y = extended(vel_y, (("sy", 1),), 2)
        diverge = behind(rim_x, 0, cx) + behind(rim_y, 1, cy)
        diverge = diverge + behind(jnp.pad(vel_z, ((0, 0), (0, 0), (2, 2))), 2, cz)
        press = press - courant * diverge
        press = press + amplitude * source_mask
        record = press.reshape(-1)[cell_index] * valid
        return ((press, vel_x, vel_y, vel_z), record)

    start = (pressure, velocity[0], velocity[1], velocity[2])
    final, records = lax.scan(advance, start, wavelet)
    press, vel_x, vel_y, vel_z = final
    summed = correlate(records, got_rows, nlag)
    total = lax.psum(summed, ("sx", "sy"))
    scale = 1.0 / math.sqrt(subs * r_dev * steps)
    return (press, jnp.stack([vel_x, vel_y, vel_z]), total * scale)


def solution(mesh):
    placed = (
        P(("shot", "sx"), "sy", None),
        P(None, ("shot", "sx"), "sy", None),
        P("sx", "sy", None),
        P(("shot", "sx", "sy"), None),
        P(("shot", "sx", "sy"), None),
        P(("shot", "sx", "sy")),
        P("shot"),
        P(),
    )
    return jax.shard_map(
        body,
        mesh=mesh,
        in_specs=placed,
        out_specs=(P(("shot", "sx"), "sy", None), P(None, ("shot", "sx"), "sy", None), P("shot")),
        check_vma=False,
    )
```

profile of v0, /device:TPU:0, one launch (start us, length us, event | category | flops | bytes accessed | tf_op | source)
XLA Modules:
  0.0 680.5 jit_solution(15407832240016842166)
XLA Ops:
  5.5 7.4 %all-to-all-start = ((f32[16,1,16]{2,1,0:T(1,128)}), f32[16,1,16]{2,1,0:T(1,128)S(1)}, u32[]{:S(2)}, u32[]{:S(2)}) async-start(f32[16,1,16]{2,1,0:T(1,128)} %all_to_all.9), calls=%async_computation | async-start | bytes 16384 | tf_op jit(solution)/shard_map/all_to_all | solution.py:84
  19.2 4.7 all-to-all-start.1
  24.1 596.5 %while.35 = (s32[]{:T(128)}, f32[16,16,128]{2,1,0:T(8,128)S(1)}, f32[16,16,128]{2,1,0:T(8,128)S(1)}, f32[16,16,128]{2,1,0:T(8,128)S(1)}, f32[16,16,128]{2,1,0:T(...) while((s32[]{:T(128)}, f32[16,16,128]{2,1,0:T(8,128)S(1)}, ...), condition=%wide.region_4.5_spmd.clone, body=%wide.region_3.4_spmd.clone.sunk | while | flops 1771522 | bytes 3710601 | solution.py:113
  24.1 3.8 collective-permute-start
  31.2 5.6 collective-permute-done.1
  41.7 26.3 %collective-permute-start.4 = (f32[2,16,128]{2,1,0:T(8,128)S(1)}, f32[2,16,128]{2,1,0:T(8,128)S(1)}, u32[]{:S(2)}, u32[]{:S(2)}) collective-permute-start(f32[2,16,128]{2,1,0:T(8,128)S(1)} %get-tuple-element.453), channel_id=1, source_target_pairs={{0,2},{2,4},{4,6},{6,8},{8,10},{10,12},{12,14},{1,3},{3,5},{5,7},{... | collective-permute-start | bytes 49160 | tf_op jit(solution)/shard_map/while/body/eval_jaxpr/ppermute | solution.py:17
  73.0 5.1 collective-permute-done.7
  80.8 13.9 %collective-permute-start = (f32[2,16,128]{2,1,0:T(8,128)S(1)}, f32[2,16,128]{2,1,0:T(8,128)S(1)}, u32[]{:S(2)}, u32[]{:S(2)}) collective-permute-start(f32[2,16,128]{2,1,0:T(8,128)S(1)} %get-tuple-element.444), channel_id=1, source_target_pairs={{0,2},{2,4},{4,6},{6,8},{8,10},{10,12},{12,14},{1,3},{3,5},{5,7},{... | collective-permute-start | bytes 49160 | tf_op jit(solution)/shard_map/while/body/eval_jaxpr/ppermute | solution.py:17
  96.1 4.2 collective-permute-done.1
  104.9 4.8 collective-permute-start.4
  121.2 4.5 collective-permute-start
  127.2 4.2 collective-permute-done.1
  143.9 3.7 collective-permute-done.7
  154.9 4.2 collective-permute-done.1
  182.5 4.2 collective-permute-done.1
  210.2 4.2 collective-permute-done.1
  237.9 4.2 collective-permute-done.1
  265.5 4.2 collective-permute-done.1
  293.2 4.2 collective-permute-done.1
  320.9 4.2 collective-permute-done.1
  348.5 4.2 collective-permute-done.1
  376.2 4.2 collective-permute-done.1
  403.9 4.2 collective-permute-done.1
  431.5 4.2 collective-permute-done.1
  459.2 4.2 collective-permute-done.1
  486.9 4.2 collective-permute-done.1
  514.5 4.2 collective-permute-done.1
  542.2 4.2 collective-permute-done.1
  569.9 4.2 collective-permute-done.1
  597.5 4.2 collective-permute-done.1
  621.4 28.3 %while.36 = (s32[]{:T(128)}, f32[1981]{0:T(1024)S(1)}, f32[20,256]{1,0:T(8,128)S(1)}, f32[256,2000]{1,0:T(8,128)S(1)}, s32[]{:T(128)}, /*index=5*/s32[]{:T(128)}) while((s32[]{:T(128)}, f32[1981]{0:T(1024)S(1)}, f32[20,256]{1,0:T(8,128)S(1)}, f32[256,2000]{1,0:T(8,128)S(1)}, s32[]{:T(128)}, /*index=5*/s32[]{:T(128)}) %tuple.92), condition=%wide.region_7.8_spmd.clone, body=%wide.region_6.7_spmd.clone.sunk | while | flops 6089597 | bytes 2130975 | solution.py:49
  649.8 30.1 %psum.7 = f32[1981]{0:T(1024)S(1)} all-reduce(f32[1981]{0:T(1024)S(1)} %get-tuple-element.228), channel_id=1, replica_groups=mesh['shot'=2,'sx'=8,'sy'=2] {'sx','sy'}, use_global_device_ids=true, to_apply=%region_8.9 | all-reduce | flops 1981 | bytes 15848 | tf_op jit(solution)/shard_map/psum | solution.py:116
  (665 shorter events, 486.2 us)
Async XLA Ops:
  5.5 13.7 %all-to-all-start = ((f32[16,1,16]{2,1,0:T(1,128)}), f32[16,1,16]{2,1,0:T(1,128)S(1)}, u32[]{:S(2)}, u32[]{:S(2)}) async-start(f32[16,1,16]{2,1,0:T(1,128)} %all_to_all.9), calls=%async_computation | async-start | bytes 16384 | tf_op jit(solution)/shard_map/all_to_all | solution.py:84
  19.2 602.3 %all-to-all-start.1 = ((f32[16,16,2000]{2,1,0:T(8,128)}), f32[16,16,2000]{2,1,0:T(8,128)S(1)}, u32[]{:S(2)}, u32[]{:S(2)}) async-start(f32[16,16,2000]{2,1,0:T(8,128)} %bitcast.52), calls=%async_computation.1 | async-start | bytes 4194304 | tf_op jit(solution)/shard_map/all_to_all | solution.py:81
  24.1 7.1 %collective-permute-start = (f32[2,16,128]{2,1,0:T(8,128)S(1)}, f32[2,16,128]{2,1,0:T(8,128)S(1)}, u32[]{:S(2)}, u32[]{:S(2)}) collective-permute-start(f32[2,16,128]{2,1,0:T(8,128)S(1)} %get-tuple-element.444), channel_id=1, source_target_pairs={{0,2},{2,4},{4,6},{6,8},{8,10},{10,12},{12,14},{1,3},{3,5},{5,7},{... | collective-permute-start | bytes 49160 | tf_op jit(solution)/shard_map/while/body/eval_jaxpr/ppermute | solution.py:17
  28.0 8.9 %collective-permute-start.1 = (f32[2,16,128]{2,1,0:T(8,128)S(1)}, f32[2,16,128]{2,1,0:T(8,128)S(1)}, u32[]{:S(2)}, u32[]{:S(2)}) collective-permute-start(f32[2,16,128]{2,1,0:T(8,128)S(1)} %get-tuple-element.446), channel_id=1, source_target_pairs={{2,0},{4,2},{6,4},{8,6},{10,8},{12,10},{14,12},{3,1},{5,3},{7,5},{... | collective-permute-start | bytes 49160 | tf_op jit(solution)/shard_map/while/body/eval_jaxpr/ppermute | solution.py:20
  41.7 31.3 %collective-permute-start.4 = (f32[2,16,128]{2,1,0:T(8,128)S(1)}, f32[2,16,128]{2,1,0:T(8,128)S(1)}, u32[]{:S(2)}, u32[]{:S(2)}) collective-permute-start(f32[2,16,128]{2,1,0:T(8,128)S(1)} %get-tuple-element.453), channel_id=1, source_target_pairs={{0,2},{2,4},{4,6},{6,8},{8,10},{10,12},{12,14},{1,3},{3,5},{5,7},{... | collective-permute-start | bytes 49160 | tf_op jit(solution)/shard_map/while/body/eval_jaxpr/ppermute | solution.py:17
  71.1 7.0 %collective-permute-start.7 = (f32[2,16,128]{2,1,0:T(8,128)S(1)}, f32[2,16,128]{2,1,0:T(8,128)S(1)}, u32[]{:S(2)}, u32[]{:S(2)}) collective-permute-start(f32[2,16,128]{2,1,0:T(8,128)S(1)} %get-tuple-element.458), channel_id=1, source_target_pairs={{2,0},{4,2},{6,4},{8,6},{10,8},{12,10},{14,12},{3,1},{5,3},{7,5},{... | collective-permute-start | bytes 49160 | tf_op jit(solution)/shard_map/while/body/eval_jaxpr/ppermute | solution.py:20
  80.8 15.3 %collective-permute-start = (f32[2,16,128]{2,1,0:T(8,128)S(1)}, f32[2,16,128]{2,1,0:T(8,128)S(1)}, u32[]{:S(2)}, u32[]{:S(2)}) collective-permute-start(f32[2,16,128]{2,1,0:T(8,128)S(1)} %get-tuple-element.444), channel_id=1, source_target_pairs={{0,2},{2,4},{4,6},{6,8},{8,10},{10,12},{12,14},{1,3},{3,5},{5,7},{... | collective-permute-start | bytes 49160 | tf_op jit(solution)/shard_map/while/body/eval_jaxpr/ppermute | solution.py:17
  94.6 5.7 collective-permute-start.1
  104.9 9.8 %collective-permute-start.4 = (f32[2,16,128]{2,1,0:T(8,128)S(1)}, f32[2,16,128]{2,1,0:T(8,128)S(1)}, u32[]{:S(2)}, u32[]{:S(2)}) collective-permute-start(f32[2,16,128]{2,1,0:T(8,128)S(1)} %get-tuple-element.453), channel_id=1, source_target_pairs={{0,2},{2,4},{4,6},{6,8},{8,10},{10,12},{12,14},{1,3},{3,5},{5,7},{... | collective-permute-start | bytes 49160 | tf_op jit(solution)/shard_map/while/body/eval_jaxpr/ppermute | solution.py:17
  121.2 6.0 collective-permute-start
  136.0 7.9 %collective-permute-start.4 = (f32[2,16,128]{2,1,0:T(8,128)S(1)}, f32[2,16,128]{2,1,0:T(8,128)S(1)}, u32[]{:S(2)}, u32[]{:S(2)}) collective-permute-start(f32[2,16,128]{2,1,0:T(8,128)S(1)} %get-tuple-element.453), channel_id=1, source_target_pairs={{0,2},{2,4},{4,6},{6,8},{8,10},{10,12},{12,14},{1,3},{3,5},{5,7},{... | collective-permute-start | bytes 49160 | tf_op jit(solution)/shard_map/while/body/eval_jaxpr/ppermute | solution.py:17
  142.0 5.7 collective-permute-start.7
  163.7 7.9 %collective-permute-start.4 = (f32[2,16,128]{2,1,0:T(8,128)S(1)}, f32[2,16,128]{2,1,0:T(8,128)S(1)}, u32[]{:S(2)}, u32[]{:S(2)}) collective-permute-start(f32[2,16,128]{2,1,0:T(8,128)S(1)} %get-tuple-element.453), channel_id=1, source_target_pairs={{0,2},{2,4},{4,6},{6,8},{8,10},{10,12},{12,14},{1,3},{3,5},{5,7},{... | collective-permute-start | bytes 49160 | tf_op jit(solution)/shard_map/while/body/eval_jaxpr/ppermute | solution.py:17
  169.6 5.7 collective-permute-start.7
  191.4 7.9 %collective-permute-start.4 = (f32[2,16,128]{2,1,0:T(8,128)S(1)}, f32[2,16,128]{2,1,0:T(8,128)S(1)}, u32[]{:S(2)}, u32[]{:S(2)}) collective-permute-start(f32[2,16,128]{2,1,0:T(8,128)S(1)} %get-tuple-element.453), channel_id=1, source_target_pairs={{0,2},{2,4},{4,6},{6,8},{8,10},{10,12},{12,14},{1,3},{3,5},{5,7},{... | collective-permute-start | bytes 49160 | tf_op jit(solution)/shard_map/while/body/eval_jaxpr/ppermute | solution.py:17
  197.3 5.7 collective-permute-start.7
  219.0 7.9 %collective-permute-start.4 = (f32[2,16,128]{2,1,0:T(8,128)S(1)}, f32[2,16,128]{2,1,0:T(8,128)S(1)}, u32[]{:S(2)}, u32[]{:S(2)}) collective-permute-start(f32[2,16,128]{2,1,0:T(8,128)S(1)} %get-tuple-element.453), channel_id=1, source_target_pairs={{0,2},{2,4},{4,6},{6,8},{8,10},{10,12},{12,14},{1,3},{3,5},{5,7},{... | collective-permute-start | bytes 49160 | tf_op jit(solution)/shard_map/while/body/eval_jaxpr/ppermute | solution.py:17
  225.0 5.7 collective-permute-start.7
  246.7 7.9 %collective-permute-start.4 = (f32[2,16,128]{2,1,0:T(8,128)S(1)}, f32[2,16,128]{2,1,0:T(8,128)S(1)}, u32[]{:S(2)}, u32[]{:S(2)}) collective-permute-start(f32[2,16,128]{2,1,0:T(8,128)S(1)} %get-tuple-element.453), channel_id=1, source_target_pairs={{0,2},{2,4},{4,6},{6,8},{8,10},{10,12},{12,14},{1,3},{3,5},{5,7},{... | collective-permute-start | bytes 49160 | tf_op jit(solution)/shard_map/while/body/eval_jaxpr/ppermute | solution.py:17
  274.4 7.9 %collective-permute-start.4 = (f32[2,16,128]{2,1,0:T(8,128)S(1)}, f32[2,16,128]{2,1,0:T(8,128)S(1)}, u32[]{:S(2)}, u32[]{:S(2)}) collective-permute-start(f32[2,16,128]{2,1,0:T(8,128)S(1)} %get-tuple-element.453), channel_id=1, source_target_pairs={{0,2},{2,4},{4,6},{6,8},{8,10},{10,12},{12,14},{1,3},{3,5},{5,7},{... | collective-permute-start | bytes 49160 | tf_op jit(solution)/shard_map/while/body/eval_jaxpr/ppermute | solution.py:17
  302.0 7.9 %collective-permute-start.4 = (f32[2,16,128]{2,1,0:T(8,128)S(1)}, f32[2,16,128]{2,1,0:T(8,128)S(1)}, u32[]{:S(2)}, u32[]{:S(2)}) collective-permute-start(f32[2,16,128]{2,1,0:T(8,128)S(1)} %get-tuple-element.453), channel_id=1, source_target_pairs={{0,2},{2,4},{4,6},{6,8},{8,10},{10,12},{12,14},{1,3},{3,5},{5,7},{... | collective-permute-start | bytes 49160 | tf_op jit(solution)/shard_map/while/body/eval_jaxpr/ppermute | solution.py:17
  329.7 7.9 %collective-permute-start.4 = (f32[2,16,128]{2,1,0:T(8,128)S(1)}, f32[2,16,128]{2,1,0:T(8,128)S(1)}, u32[]{:S(2)}, u32[]{:S(2)}) collective-permute-start(f32[2,16,128]{2,1,0:T(8,128)S(1)} %get-tuple-element.453), channel_id=1, source_target_pairs={{0,2},{2,4},{4,6},{6,8},{8,10},{10,12},{12,14},{1,3},{3,5},{5,7},{... | collective-permute-start | bytes 49160 | tf_op jit(solution)/shard_map/while/body/eval_jaxpr/ppermute | solution.py:17
  357.4 7.9 %collective-permute-start.4 = (f32[2,16,128]{2,1,0:T(8,128)S(1)}, f32[2,16,128]{2,1,0:T(8,128)S(1)}, u32[]{:S(2)}, u32[]{:S(2)}) collective-permute-start(f32[2,16,128]{2,1,0:T(8,128)S(1)} %get-tuple-element.453), channel_id=1, source_target_pairs={{0,2},{2,4},{4,6},{6,8},{8,10},{10,12},{12,14},{1,3},{3,5},{5,7},{... | collective-permute-start | bytes 49160 | tf_op jit(solution)/shard_map/while/body/eval_jaxpr/ppermute | solution.py:17
  385.0 7.9 %collective-permute-start.4 = (f32[2,16,128]{2,1,0:T(8,128)S(1)}, f32[2,16,128]{2,1,0:T(8,128)S(1)}, u32[]{:S(2)}, u32[]{:S(2)}) collective-permute-start(f32[2,16,128]{2,1,0:T(8,128)S(1)} %get-tuple-element.453), channel_id=1, source_target_pairs={{0,2},{2,4},{4,6},{6,8},{8,10},{10,12},{12,14},{1,3},{3,5},{5,7},{... | collective-permute-start | bytes 49160 | tf_op jit(solution)/shard_map/while/body/eval_jaxpr/ppermute | solution.py:17
  412.7 7.9 %collective-permute-start.4 = (f32[2,16,128]{2,1,0:T(8,128)S(1)}, f32[2,16,128]{2,1,0:T(8,128)S(1)}, u32[]{:S(2)}, u32[]{:S(2)}) collective-permute-start(f32[2,16,128]{2,1,0:T(8,128)S(1)} %get-tuple-element.453), channel_id=1, source_target_pairs={{0,2},{2,4},{4,6},{6,8},{8,10},{10,12},{12,14},{1,3},{3,5},{5,7},{... | collective-permute-start | bytes 49160 | tf_op jit(solution)/shard_map/while/body/eval_jaxpr/ppermute | solution.py:17
  440.4 7.9 %collective-permute-start.4 = (f32[2,16,128]{2,1,0:T(8,128)S(1)}, f32[2,16,128]{2,1,0:T(8,128)S(1)}, u32[]{:S(2)}, u32[]{:S(2)}) collective-permute-start(f32[2,16,128]{2,1,0:T(8,128)S(1)} %get-tuple-element.453), channel_id=1, source_target_pairs={{0,2},{2,4},{4,6},{6,8},{8,10},{10,12},{12,14},{1,3},{3,5},{5,7},{... | collective-permute-start | bytes 49160 | tf_op jit(solution)/shard_map/while/body/eval_jaxpr/ppermute | solution.py:17
  468.0 7.9 %collective-permute-start.4 = (f32[2,16,128]{2,1,0:T(8,128)S(1)}, f32[2,16,128]{2,1,0:T(8,128)S(1)}, u32[]{:S(2)}, u32[]{:S(2)}) collective-permute-start(f32[2,16,128]{2,1,0:T(8,128)S(1)} %get-tuple-element.453), channel_id=1, source_target_pairs={{0,2},{2,4},{4,6},{6,8},{8,10},{10,12},{12,14},{1,3},{3,5},{5,7},{... | collective-permute-start | bytes 49160 | tf_op jit(solution)/shard_map/while/body/eval_jaxpr/ppermute | solution.py:17
  495.7 7.9 %collective-permute-start.4 = (f32[2,16,128]{2,1,0:T(8,128)S(1)}, f32[2,16,128]{2,1,0:T(8,128)S(1)}, u32[]{:S(2)}, u32[]{:S(2)}) collective-permute-start(f32[2,16,128]{2,1,0:T(8,128)S(1)} %get-tuple-element.453), channel_id=1, source_target_pairs={{0,2},{2,4},{4,6},{6,8},{8,10},{10,12},{12,14},{1,3},{3,5},{5,7},{... | collective-permute-start | bytes 49160 | tf_op jit(solution)/shard_map/while/body/eval_jaxpr/ppermute | solution.py:17
  523.4 7.9 %collective-permute-start.4 = (f32[2,16,128]{2,1,0:T(8,128)S(1)}, f32[2,16,128]{2,1,0:T(8,128)S(1)}, u32[]{:S(2)}, u32[]{:S(2)}) collective-permute-start(f32[2,16,128]{2,1,0:T(8,128)S(1)} %get-tuple-element.453), channel_id=1, source_target_pairs={{0,2},{2,4},{4,6},{6,8},{8,10},{10,12},{12,14},{1,3},{3,5},{5,7},{... | collective-permute-start | bytes 49160 | tf_op jit(solution)/shard_map/while/body/eval_jaxpr/ppermute | solution.py:17
  551.0 7.9 %collective-permute-start.4 = (f32[2,16,128]{2,1,0:T(8,128)S(1)}, f32[2,16,128]{2,1,0:T(8,128)S(1)}, u32[]{:S(2)}, u32[]{:S(2)}) collective-permute-start(f32[2,16,128]{2,1,0:T(8,128)S(1)} %get-tuple-element.453), channel_id=1, source_target_pairs={{0,2},{2,4},{4,6},{6,8},{8,10},{10,12},{12,14},{1,3},{3,5},{5,7},{... | collective-permute-start | bytes 49160 | tf_op jit(solution)/shard_map/while/body/eval_jaxpr/ppermute | solution.py:17
  578.7 7.9 %collective-permute-start.4 = (f32[2,16,128]{2,1,0:T(8,128)S(1)}, f32[2,16,128]{2,1,0:T(8,128)S(1)}, u32[]{:S(2)}, u32[]{:S(2)}) collective-permute-start(f32[2,16,128]{2,1,0:T(8,128)S(1)} %get-tuple-element.453), channel_id=1, source_target_pairs={{0,2},{2,4},{4,6},{6,8},{8,10},{10,12},{12,14},{1,3},{3,5},{5,7},{... | collective-permute-start | bytes 49160 | tf_op jit(solution)/shard_map/while/body/eval_jaxpr/ppermute | solution.py:17
  606.4 7.9 %collective-permute-start.4 = (f32[2,16,128]{2,1,0:T(8,128)S(1)}, f32[2,16,128]{2,1,0:T(8,128)S(1)}, u32[]{:S(2)}, u32[]{:S(2)}) collective-permute-start(f32[2,16,128]{2,1,0:T(8,128)S(1)} %get-tuple-element.453), channel_id=1, source_target_pairs={{0,2},{2,4},{4,6},{6,8},{8,10},{10,12},{12,14},{1,3},{3,5},{5,7},{... | collective-permute-start | bytes 49160 | tf_op jit(solution)/shard_map/while/body/eval_jaxpr/ppermute | solution.py:17
  (135 other events, 571.4 us)
where the time goes:
time: 685 us; the launch traced here: 680 us
  starting transfers between devices  334 us (49%)
  waiting for transfers between devices  202 us (29%)
  local copies, waits for them, and re-layouts  54.2 us (8%)
  blocking collectives  30.1 us (4%)
  matrix products  28.1 us (4%)
  other arithmetic  26.7 us (4%)
    ppermute x80, starting transfers between devices, extended(): lax.ppermute(lax.slice_in_dim(block, block.shape[dim] - width, None, axis...  219 us
    ppermute x80, waiting for transfers between devices, extended(): lax.ppermute(lax.slice_in_dim(block, 0, width, axis=dim), axis, backward)  196 us
    ppermute x80, starting transfers between devices, extended(): lax.ppermute(lax.slice_in_dim(block, 0, width, axis=dim), axis, backward)  103 us
    gather x20, local copies, waits for them, and re-layouts, advance(): record = press.reshape(-1)[cell_index] * valid  34.4 us
    psum x1, blocking collectives, body(): total = lax.psum(summed, ('sx', 'sy'))  30.1 us
    dot_general x20, matrix products, add_step(): return summed + jnp.dot(line, window, precision=lax.Precision.HIGHEST)  28.1 us
    add x20, other arithmetic, advance(): press = press + amplitude * source_mask  17.4 us
  transfers between devices with their start and end apart: 162, of which 81 were waited for; matrix products, arithmetic and copies ran while one was open for 11% of the time, Pallas kernels for 0%

commit v1 on v0

v1 whole, which is shorter than its diff:
```python
import functools
import math

import jax
import jax.numpy as jnp
from jax import lax
from jax.experimental import pallas as pl
from jax.experimental.pallas import tpu as pltpu
from jax.sharding import PartitionSpec as P

c_one = 9.0 / 8.0
c_two = -1.0 / 24.0
HALO = 3
SIDE = 8


def pieces(value, count):
    parts = []
    for _ in range(count):
        part = value.astype(jnp.bfloat16)
        parts.append(part)
        value = value - part.astype(jnp.float32)
    return parts


def slope(a, b, c, d):
    return c_one * (a - b) + c_two * (c - d)


def shifted(f, k, axis):
    count = f.shape[axis]
    return pltpu.roll(f, (-k) % count, axis)


def shifted_z(f, k):
    count = f.shape[-1]
    place = lax.broadcasted_iota(jnp.int32, f.shape, f.ndim - 1)
    keep = place < count - k if k > 0 else place >= -k
    return jnp.where(keep, shifted(f, k, f.ndim - 1), 0.0)


def kernel(
    count_x,
    count_y,
    cap,
    press_ref,
    vel_ref,
    cour_ref,
    obs_ref,
    owner_ref,
    cell_ref,
    src_ref,
    wave_ref,
    press_out,
    vel_out,
    xc_out,
    field,
    speed,
    edge_x,
    edge_y,
    base,
    mark,
    now,
    codes_out,
    codes_in,
    rows_hot,
    lane_hot,
    records,
    returned,
    table,
    sums,
    halo_send,
    halo_recv,
    once_send,
    once_recv,
    swap_send,
    swap_recv,
):
    cx, cy, cz = press_ref.shape
    r_dev, nt = obs_ref.shape
    steps = wave_ref.shape[0]
    nlag = nt - steps + 1
    subs = count_x * count_y
    slots = subs * cap
    ix = lax.axis_index("sx")
    iy = lax.axis_index("sy")
    me = ix * count_y + iy
    inner = pl.ds(SIDE, cy)

    def place_of(peer):
        return {"sx": peer // count_y, "sy": peer % count_y}

    def peer_at(k):
        return lax.rem(me + k, subs)

    field[...] = jnp.zeros_like(field)
    speed[...] = jnp.zeros_like(speed)
    edge_x[...] = jnp.zeros_like(edge_x)
    edge_y[...] = jnp.zeros_like(edge_y)

    barrier = pltpu.get_barrier_semaphore()

    def greet(k, carry):
        pl.semaphore_signal(
            barrier, inc=1, device_id=place_of(peer_at(k)), device_id_type=pl.DeviceIdType.MESH
        )
        return carry

    lax.fori_loop(1, subs, greet, 0)

    low = {"sx": ix - 1}
    high = {"sx": ix + 1}
    beside = {"sy": 1 - iy}
    has_low = ix > 0
    has_high = ix < count_x - 1

    def remote(src, dst, send, recv, device):
        return pltpu.make_async_remote_copy(
            src_ref=src,
            dst_ref=dst,
            send_sem=send,
            recv_sem=recv,
            device_id=device,
            device_id_type=pl.DeviceIdType.MESH,
        )

    y_from = pl.multiple_of(SIDE * (1 - iy), SIDE)
    y_to = pl.multiple_of((SIDE + cy) * iy, SIDE)
    y_rows = pl.ds(y_from + SIDE, SIDE)
    y_land = pl.ds(y_to, SIDE)
    y_own = pl.ds(y_from, SIDE)
    mid = pl.ds(HALO, cx)
    top = pl.ds(HALO + cx, HALO)
    bottom = pl.ds(0, HALO)

    def to_low(b):
        return remote(
            field.at[b, pl.ds(HALO, HALO), inner],
            field.at[b, top, inner],
            halo_send.at[0, b],
            halo_recv.at[0, b],
            low,
        )

    def to_high(b):
        return remote(
            field.at[b, pl.ds(cx, HALO), inner],
            field.at[b, bottom, inner],
            halo_send.at[1, b],
            halo_recv.at[1, b],
            high,
        )

    def to_side(b):
        return remote(
            field.at[b, mid, y_rows],
            field.at[b, mid, y_land],
            halo_send.at[2, b],
            halo_recv.at[2, b],
            beside,
        )

    def once_low():
        part = pl.ds(0, HALO)
        return [
            remote(cour_ref.at[part], speed.at[top, inner], once_send.at[0], once_recv.at[0], low),
            remote(vel_ref.at[0, part], edge_x.at[top], once_send.at[1], once_recv.at[1], low),
        ]

    def once_high():
        part = pl.ds(cx - HALO, HALO)
        return [
            remote(cour_ref.at[part], speed.at[bottom, inner], once_send.at[2], once_recv.at[2], high),
            remote(vel_ref.at[0, part], edge_x.at[bottom], once_send.at[3], once_recv.at[3], high),
        ]

    def once_side():
        return [
            remote(
                cour_ref.at[:, y_own], speed.at[mid, y_land], once_send.at[4], once_recv.at[4], beside
            ),
            remote(
                vel_ref.at[1, :, y_own], edge_y.at[:, y_land], once_send.at[5], once_recv.at[5], beside
            ),
        ]

    lane = lax.broadcasted_iota(jnp.int32, (r_dev, r_dev), 1)
    row = lax.broadcasted_iota(jnp.int32, (r_dev, r_dev), 0)
    down = jnp.broadcast_to(owner_ref[...], (r_dev, r_dev)).astype(jnp.float32)
    across = jnp.sum(jnp.where(lane == row, down, 0.0), axis=0, keepdims=True)
    earlier = jnp.where((down == across) & (row < lane), 1.0, 0.0)
    rank = jnp.sum(earlier, axis=0, keepdims=True)
    spot = (across * float(cap) + rank).astype(jnp.int32)
    slot_id = lax.broadcasted_iota(jnp.int32, (slots, r_dev), 0)
    chosen = slot_id == spot
    code = (cell_ref[...] + 1).astype(jnp.float32)
    packed = jnp.sum(jnp.where(chosen, code, 0.0), axis=1, keepdims=True)
    codes_out[...] = jnp.broadcast_to(packed, codes_out.shape)

    field[0, HALO : HALO + cx, SIDE : SIDE + cy, :] = press_ref[...]
    speed[HALO : HALO + cx, SIDE : SIDE + cy, :] = cour_ref[...]
    edge_x[HALO : HALO + cx] = vel_ref[0]
    edge_y[:, SIDE : SIDE + cy, :] = vel_ref[1]
    now[...] = press_ref[...]
    records[...] = jnp.zeros_like(records)

    pl.semaphore_wait(barrier, subs - 1)

    @pl.when(has_low)
    def _():
        to_low(0).start()
        for copy in once_low():
            copy.start()

    @pl.when(has_high)
    def _():
        to_high(0).start()
        for copy in once_high():
            copy.start()

    to_side(0).start()
    for copy in once_side():
        copy.start()

    def swap(stage, source, landing, k):
        peer = peer_at(k)
        return remote(
            source.at[pl.ds(pl.multiple_of(peer * cap, 8), cap)],
            landing.at[pl.ds(pl.multiple_of(me * cap, 8), cap)],
            swap_send.at[stage, k],
            swap_recv.at[stage, k],
            place_of(peer),
        )

    def share(k):
        return remote(
            sums.at[me], sums.at[me], swap_send.at[2, k], swap_recv.at[2, k], place_of(peer_at(k))
        )

    def each(action):
        def one(k, carry):
            action(k)
            return carry

        lax.fori_loop(1, subs, one, 0)

    each(lambda k: swap(0, codes_out, codes_in, k).start())
    own = pl.ds(pl.multiple_of(me * cap, 8), cap)
    codes_in[own, :] = codes_out[own, :]

    shape = (cx, cy, cz)
    gx = lax.broadcasted_iota(jnp.int32, shape, 0) + ix * cx
    gy = lax.broadcasted_iota(jnp.int32, shape, 1) + iy * cy
    gz = lax.broadcasted_iota(jnp.int32, shape, 2)
    mark[...] = jnp.where((gx * (cy * count_y) + gy) * cz + gz == src_ref[0], 1.0, 0.0)

    @pl.when(has_low)
    def _():
        for copy in once_low():
            copy.wait_send()
        for copy in once_high():
            copy.wait_recv()

    @pl.when(has_high)
    def _():
        for copy in once_high():
            copy.wait_send()
        for copy in once_low():
            copy.wait_recv()

    for copy in once_side():
        copy.wait()

    fx = edge_x[1 : cx + 4]
    fy = edge_y[...]
    fz = vel_ref[2]
    spread = slope(fx[2 : 2 + cx], fx[1 : 1 + cx], fx[3 : 3 + cx], fx[0:cx])
    spread_y = slope(fy, shifted(fy, -1, 1), shifted(fy, 1, 1), shifted(fy, -2, 1))
    spread = spread + spread_y[:, SIDE : SIDE + cy]
    spread = spread + slope(fz, shifted_z(fz, -1), shifted_z(fz, 1), shifted_z(fz, -2))
    base[...] = cour_ref[...] * spread

    def grads(b, first, last):
        n = last - first
        fx = field[b, first : last + 2 * HALO, SIDE : SIDE + cy, :]
        m = n + 3
        grad_x = speed[first + 1 : last + 4, SIDE : SIDE + cy, :] * slope(
            fx[2 : 2 + m], fx[1 : 1 + m], fx[3 : 3 + m], fx[0:m]
        )
        fy = field[b, first + HALO : last + HALO]
        grad_y = speed[first + HALO : last + HALO] * slope(
            shifted(fy, 1, 1), fy, shifted(fy, 2, 1), shifted(fy, -1, 1)
        )
        fz = fy[:, SIDE : SIDE + cy]
        cour = cour_ref[first:last]
        grad_z = cour * slope(shifted_z(fz, 1), fz, shifted_z(fz, 2), shifted_z(fz, -1))
        return (grad_x, grad_y, grad_z, fz, cour)

    def update(b, first, last, amplitude):
        n = last - first
        grad_x, grad_y, grad_z, total, cour = grads(b, first, last)
        acc = slope(grad_x[2 : 2 + n], grad_x[1 : 1 + n], grad_x[3 : 3 + n], grad_x[0:n])
        acc_y = slope(
            grad_y, shifted(grad_y, -1, 1), shifted(grad_y, 1, 1), shifted(grad_y, -2, 1)
        )
        acc = acc + acc_y[:, SIDE : SIDE + cy]
        acc = acc + slope(
            grad_z, shifted_z(grad_z, -1), shifted_z(grad_z, 1), shifted_z(grad_z, -2)
        )
        fresh = now[first:last] + (cour * acc - base[first:last]) + amplitude * mark[first:last]
        now[first:last] = fresh
        field[1 - b, first + HALO : last + HALO, SIDE : SIDE + cy, :] = total + fresh

    def listen():
        each(lambda k: swap(0, codes_out, codes_in, k).wait())
        cell = codes_in[...].astype(jnp.int32) - 1
        bits = cz.bit_length() - 1
        cell_row = lax.shift_right_arithmetic(cell, jnp.full_like(cell, bits))
        cell_lane = cell & (cz - 1)
        lanes = lax.broadcasted_iota(jnp.int32, (slots, cz), 1)
        lane_hot[...] = jnp.where(cell_lane == lanes, 1.0, 0.0)
        for j in range(cx * cy // cz):
            rows_hot[:, j * cz : (j + 1) * cz] = jnp.where(
                cell_row == lanes + j * cz, 1.0, 0.0
            ).astype(jnp.bfloat16)

    def record(t):
        flat = now[...].reshape(cx * cy, cz)
        picked = jnp.zeros((slots, cz), jnp.float32)
        for part in pieces(flat, 3):
            picked = picked + jnp.dot(rows_hot[...], part, preferred_element_type=jnp.float32)
        value = jnp.sum(picked * lane_hot[...], axis=1, keepdims=True)
        lanes = lax.broadcasted_iota(jnp.int32, (slots, cz), 1)
        records[...] = jnp.where(lanes == t, value, records[...])

    listen()

    def advance(t, carry):
        b = lax.rem(t, 2)
        more = t < steps - 1

        @pl.when(has_low)
        def _():
            to_low(b).wait_send()
            to_high(b).wait_recv()

        @pl.when(has_high)
        def _():
            to_high(b).wait_send()
            to_low(b).wait_recv()

        to_side(b).wait()
        amplitude = wave_ref[t]
        update(b, 0, HALO, amplitude)

        @pl.when(has_low & more)
        def _():
            to_low(1 - b).start()

        update(b, cx - HALO, cx, amplitude)

        @pl.when(has_high & more)
        def _():
            to_high(1 - b).start()

        update(b, HALO, cx - HALO, amplitude)

        @pl.when(more)
        def _():
            to_side(1 - b).start()

        record(t)
        return carry

    lax.fori_loop(0, steps, advance, 0)

    each(lambda k: swap(1, records, returned, k).start())
    returned[own, :] = records[own, :]

    grad_x, grad_y, grad_z, _, _ = grads((steps - 1) % 2, 0, cx)
    vel_out[0] = vel_ref[0] - grad_x[2 : 2 + cx]
    vel_out[1] = vel_ref[1] - grad_y[:, SIDE : SIDE + cy]
    vel_out[2] = vel_ref[2] - grad_z
    press_out[...] = now[...]

    each(lambda k: swap(1, records, returned, k).wait())
    height = table.shape[0]
    by_step = jnp.transpose(returned[...])[0:height]
    hot = jnp.where(chosen, 1.0, 0.0).astype(jnp.bfloat16)
    syn = jnp.zeros((height, r_dev), jnp.float32)
    for part in pieces(by_step, 3):
        syn = syn + jnp.dot(part, hot, preferred_element_type=jnp.float32)
    table[...] = jnp.zeros_like(table)
    table[:, 0:nt] = jnp.dot(
        syn, obs_ref[...], precision=lax.Precision.HIGHEST, preferred_element_type=jnp.float32
    )
    lines = table[...]
    step_id = lax.broadcasted_iota(jnp.int32, lines.shape, 0)
    for bit in range((steps - 1).bit_length()):
        lines = jnp.where((step_id & (1 << bit)) != 0, shifted(lines, 1 << bit, 1), lines)
    scale = 1.0 / math.sqrt(subs * r_dev * steps)
    sums[me] = jnp.sum(lines, axis=0, keepdims=True) * scale
    each(lambda k: share(k).start())
    each(lambda k: share(k).wait())
    xc_out[...] = jnp.sum(sums[...], axis=0)


def body(pressure, velocity, courant, observed, rec_owner, rec_cell, src_pos, wavelet):
    cx, cy, cz = pressure.shape
    count_x = lax.axis_size("sx")
    count_y = lax.axis_size("sy")
    subs = count_x * count_y
    r_dev, nt = observed.shape
    steps = wavelet.shape[0]
    nlag = nt - steps + 1
    cap = -(-max(2, 2 * r_dev // subs) // 8) * 8
    slots = subs * cap
    wide = -(-nt // 128) * 128
    height = -(-steps // 8) * 8
    deep = cx + 2 * HALO
    tall = cy + 2 * SIDE
    f32 = jnp.float32
    vmem = pl.BlockSpec(memory_space=pltpu.VMEM)
    smem = pl.BlockSpec(memory_space=pltpu.SMEM)
    press, vel, xc = pl.pallas_call(
        functools.partial(kernel, count_x, count_y, cap),
        out_shape=(
            jax.ShapeDtypeStruct((cx, cy, cz), f32),
            jax.ShapeDtypeStruct((3, cx, cy, cz), f32),
            jax.ShapeDtypeStruct((1, wide), f32),
        ),
        in_specs=[vmem] * 6 + [smem] * 2,
        out_specs=(vmem,) * 3,
        scratch_shapes=[
            pltpu.VMEM((2, deep, tall, cz), f32),
            pltpu.VMEM((deep, tall, cz), f32),
            pltpu.VMEM((deep, cy, cz), f32),
            pltpu.VMEM((cx, tall, cz), f32),
            pltpu.VMEM((cx, cy, cz), f32),
            pltpu.VMEM((cx, cy, cz), f32),
            pltpu.VMEM((cx, cy, cz), f32),
            pltpu.VMEM((slots, cz), f32),
            pltpu.VMEM((slots, cz), f32),
            pltpu.VMEM((slots, cx * cy), jnp.bfloat16),
            pltpu.VMEM((slots, cz), f32),
            pltpu.VMEM((slots, cz), f32),
            pltpu.VMEM((slots, cz), f32),
            pltpu.VMEM((height, wide), f32),
            pltpu.VMEM((subs, 1, wide), f32),
            pltpu.SemaphoreType.DMA((3, 2)),
            pltpu.SemaphoreType.DMA((3, 2)),
            pltpu.SemaphoreType.DMA((6,)),
            pltpu.SemaphoreType.DMA((6,)),
            pltpu.SemaphoreType.DMA((3, subs)),
            pltpu.SemaphoreType.DMA((3, subs)),
        ],
        compiler_params=pltpu.CompilerParams(
            collective_id=0, has_side_effects=True, vmem_limit_bytes=40 * 2**20
        ),
    )(
        pressure,
        velocity,
        courant,
        observed,
        rec_owner,
        rec_cell.reshape(1, r_dev),
        src_pos,
        wavelet,
    )
    return (press, vel, xc[0, :nlag])


def solution(mesh):
    placed = (
        P(("shot", "sx"), "sy", None),
        P(None, ("shot", "sx"), "sy", None),
        P("sx", "sy", None),
        P(("shot", "sx", "sy"), None),
        P(("shot", "sx", "sy"), None),
        P(("shot", "sx", "sy")),
        P("shot"),
        P(),
    )
    return jax.shard_map(
        body,
        mesh=mesh,
        in_specs=placed,
        out_specs=(P(("shot", "sx"), "sy", None), P(None, ("shot", "sx"), "sy", None), P("shot")),
        check_vma=False,
    )
```

time: 685 us -> 99.4 us (0.15)
  starting transfers between devices: 334 us -> 0 us
  waiting for transfers between devices: 202 us -> 0 us
  Pallas kernels: 0 us -> 93.4 us
  local copies, waits for them, and re-layouts: 54.2 us -> 4.4 us
  blocking collectives: 30.1 us -> 0 us
  matrix products: 28.1 us -> 0 us
  other arithmetic: 26.7 us -> 0 us
    ppermute x160 -> x0, starting transfers between devices: 322 us -> none  [the longest x80 219 us: extended(): lax.ppermute(lax.slice_in_dim(block, block.shape[dim] - width, None, axis...]
    ppermute x160 -> x0, waiting for transfers between devices: 201 us -> none  [the longest x80 196 us: extended(): lax.ppermute(lax.slice_in_dim(block, 0, width, axis=dim), axis, backward)]
    pallas_call x0 -> x1, Pallas kernels: none -> 93.4 us  [body(): pl.pallas_call(functools.partial(kernel, count_x, count_y, cap), out_shap...]
    gather x20 -> x0, local copies, waits for them, and re-layouts: 34.4 us -> none  [advance(): record = press.reshape(-1)[cell_index] * valid]
    psum x1 -> x0, blocking collectives: 30.1 us -> none  [body(): total = lax.psum(summed, ('sx', 'sy'))]
    dot_general x20 -> x0, matrix products: 28.1 us -> none  [add_step(): return summed + jnp.dot(line, window, precision=lax.Precision.HIGHEST)]
    add x40 -> x0, other arithmetic: 17.6 us -> none  [the longest x20 17.4 us: advance(): press = press + amplitude * source_mask]
    all_to_all x2 -> x0, starting transfers between devices: 12 us -> none  [the longest x1 7.36 us: body(): lax.all_to_all(cell_buf.reshape(subs, cap), ('sx', 'sy'), split_axis=0, c...]
  transfers between devices with their start and end apart: 162 -> 0, of which waited for: 81 -> 0; matrix products, arithmetic and copies ran while one was open for 11% -> 0% of each run, Pallas kernels for 0% -> 0%
where the time goes in v1:
time: 99.4 us; the launch traced here: 99.2 us
  Pallas kernels  93.4 us (94%)
  local copies, waits for them, and re-layouts  4.4 us (4%)
  between operations  1.38 us (1%)
    pallas_call x1, Pallas kernels, body(): pl.pallas_call(functools.partial(kernel, count_x, count_y, cap), out_shap...  93.4 us
    unnamed x17, local copies, waits for them, and re-layouts  4.4 us

profile of v1, /device:TPU:0, one launch (start us, length us, event | category | flops | bytes accessed | tf_op | source)
XLA Modules:
  0.0 99.2 jit_solution(5536987941100380760)
XLA Ops:
  1.3 0.0 copy-start.5
  1.3 0.6 copy-done.5
  1.9 0.1 copy.12.owner_ref
  2.0 0.0 copy-start
  2.1 0.0 copy-start.1
  2.1 0.0 copy-start.2
  2.1 0.0 copy-start.3
  2.1 0.0 copy-start.4
  2.1 1.6 %copy.11.obs_ref = f32[128,2000]{1,0:T(8,128)S(1)} copy(f32[128,2000]{0,1:T(8,128)} %param.11) | data formatting | bytes 2048000 | tf_op args[3]
  3.7 0.0 copy-done
  3.7 0.0 copy-done.1
  3.7 0.0 copy-done.2
  3.7 0.0 copy-done.3
  3.8 0.0 copy-done.4
  3.8 93.4 %shard_map.103 = (f32[16,16,128]{2,1,0:T(8,128)S(1)}, f32[3,16,16,128]{3,2,1,0:T(8,128)S(1)}, f32[1,2048]{1,0:T(1,128)S(1)}) custom-call(f32[16,16,128]{2,1,0:T(8,128)S(1)} %copy-done.1, f32[3,16,16,128]{3,2,1,0:T(8,128)S(1)} %copy-done, f32[16,16,128]{2,1,0:T(8,128)S(1)} %copy-done.2, f32[128,2000]{1,0:T(8,128)S(1)} %copy.11.obs_ref, ...), custom_call_target="tpu_custom_call" | custom-call | tf_op jit(solution)/shard_map/pallas_call | solution.py:425
  97.2 0.7 copy.17
  97.9 0.7 copy.18
  98.6 0.6 copy.19
Async XLA Ops:
  1.3 0.7 copy-start.5
  2.0 1.7 %copy-start = (f32[3,16,16,128]{3,2,1,0:T(8,128)S(1)}, f32[3,16,16,128]{3,2,1,0:T(8,128)}, u32[]{:S(2)}) copy-start(f32[3,16,16,128]{3,2,1,0:T(8,128)} %vel_ref.1) | copy-start | bytes 1179652
  2.1 1.7 %copy-start.1 = (f32[16,16,128]{2,1,0:T(8,128)S(1)}, f32[16,16,128]{2,1,0:T(8,128)}, u32[]{:S(2)}) copy-start(f32[16,16,128]{2,1,0:T(8,128)} %press_ref.1) | copy-start | bytes 393220
  2.1 1.7 %copy-start.2 = (f32[16,16,128]{2,1,0:T(8,128)S(1)}, f32[16,16,128]{2,1,0:T(8,128)}, u32[]{:S(2)}) copy-start(f32[16,16,128]{2,1,0:T(8,128)} %cour_ref.1) | copy-start | bytes 393220
  2.1 1.7 %copy-start.3 = (s32[128]{0:T(128)S(1)}, s32[128]{0:T(128)}, u32[]{:S(2)}) copy-start(s32[128]{0:T(128)} %param.13) | copy-start | bytes 1540
  2.1 1.7 %copy-start.4 = (f32[20]{0:T(128)S(1)}, f32[20]{0:T(128)}, u32[]{:S(2)}) copy-start(f32[20]{0:T(128)} %wave_ref.1) | copy-start | bytes 244

commit v2 on v1

--- a/solution.py
+++ b/solution.py
@@ -46,7 +46,7 @@
     press_ref,
     vel_ref,
     cour_ref,
-    obs_ref,
+    obs_far,
     owner_ref,
     cell_ref,
     src_ref,
@@ -75,6 +75,8 @@
     once_recv,
     swap_send,
     swap_recv,
+    obs_ref,
+    obs_sem,
 ):
     cx, cy, cz = press_ref.shape
     r_dev, nt = obs_ref.shape
@@ -93,6 +95,8 @@
     def peer_at(k):
         return lax.rem(me + k, subs)
 
+    fetch = pltpu.make_async_copy(obs_far, obs_ref, obs_sem.at[0])
+    fetch.start()
     field[...] = jnp.zeros_like(field)
     speed[...] = jnp.zeros_like(speed)
     edge_x[...] = jnp.zeros_like(edge_x)
@@ -333,30 +337,29 @@
         lanes = lax.broadcasted_iota(jnp.int32, (slots, cz), 1)
         records[...] = jnp.where(lanes == t, value, records[...])
 
-    listen()
-
     def advance(t, carry):
         b = lax.rem(t, 2)
         more = t < steps - 1
+
+        to_side(b).wait()
+        amplitude = wave_ref[t]
 
         @pl.when(has_low)
         def _():
             to_low(b).wait_send()
             to_high(b).wait_recv()
 
+        update(b, 0, HALO, amplitude)
+
+        @pl.when(has_low & more)
+        def _():
+            to_low(1 - b).start()
+
         @pl.when(has_high)
         def _():
             to_high(b).wait_send()
             to_low(b).wait_recv()
 
-        to_side(b).wait()
-        amplitude = wave_ref[t]
-        update(b, 0, HALO, amplitude)
-
-        @pl.when(has_low & more)
-        def _():
-            to_low(1 - b).start()
-
         update(b, cx - HALO, cx, amplitude)
 
         @pl.when(has_high & more)
@@ -368,6 +371,10 @@
         @pl.when(more)
         def _():
             to_side(1 - b).start()
+
+        @pl.when(t == 0)
+        def _():
+            listen()
 
         record(t)
         return carry
@@ -384,6 +391,7 @@
     press_out[...] = now[...]
 
     each(lambda k: swap(1, records, returned, k).wait())
+    fetch.wait()
     height = table.shape[0]
     by_step = jnp.transpose(returned[...])[0:height]
     hot = jnp.where(chosen, 1.0, 0.0).astype(jnp.bfloat16)
@@ -429,7 +437,7 @@
             jax.ShapeDtypeStruct((3, cx, cy, cz), f32),
             jax.ShapeDtypeStruct((1, wide), f32),
         ),
-        in_specs=[vmem] * 6 + [smem] * 2,
+        in_specs=[vmem] * 3 + [pl.BlockSpec(memory_space=pl.ANY)] + [vmem] * 2 + [smem] * 2,
         out_specs=(vmem,) * 3,
         scratch_shapes=[
             pltpu.VMEM((2, deep, tall, cz), f32),
@@ -453,6 +461,8 @@
             pltpu.SemaphoreType.DMA((6,)),
             pltpu.SemaphoreType.DMA((3, subs)),
             pltpu.SemaphoreType.DMA((3, subs)),
+            pltpu.VMEM((r_dev, nt), f32),
+            pltpu.SemaphoreType.DMA((1,)),
         ],
         compiler_params=pltpu.CompilerParams(
             collective_id=0, has_side_effects=True, vmem_limit_bytes=40 * 2**20

time: 99.4 us -> 97.2 us (0.978)
  Pallas kernels: 93.4 us -> 91.3 us
    pallas_call x1, Pallas kernels: 93.4 us -> 91.3 us  [body(): pl.pallas_call(functools.partial(kernel, count_x, count_y, cap), out_shap...]
where the time goes in v2:
time: 97.2 us; the launch traced here: 97.1 us
  Pallas kernels  91.3 us (94%)
  local copies, waits for them, and re-layouts  4.4 us (5%)
  between operations  1.38 us (1%)
    pallas_call x1, Pallas kernels, body(): pl.pallas_call(functools.partial(kernel, count_x, count_y, cap), out_shap...  91.3 us
    unnamed x17, local copies, waits for them, and re-layouts  4.4 us

profile of v2, /device:TPU:0, one launch (start us, length us, event | category | flops | bytes accessed | tf_op | source)
XLA Modules:
  0.0 97.1 jit_solution(15276694981066265067)
XLA Ops:
  1.3 0.0 copy-start.5
  1.3 0.6 copy-done.5
  1.9 0.1 copy.12.owner_ref
  2.0 0.0 copy-start
  2.1 0.0 copy-start.1
  2.1 0.0 copy-start.2
  2.1 0.0 copy-start.3
  2.1 0.0 copy-start.4
  2.1 1.6 %copy.11.obs_far = f32[128,2000]{1,0:T(8,128)S(1)} copy(f32[128,2000]{0,1:T(8,128)} %param.11) | data formatting | bytes 2048000 | tf_op args[3]
  3.7 0.0 copy-done
  3.7 0.0 copy-done.1
  3.7 0.0 copy-done.2
  3.7 0.0 copy-done.3
  3.8 0.0 copy-done.4
  3.8 91.3 %shard_map.103 = (f32[16,16,128]{2,1,0:T(8,128)S(1)}, f32[3,16,16,128]{3,2,1,0:T(8,128)S(1)}, f32[1,2048]{1,0:T(1,128)S(1)}) custom-call(f32[16,16,128]{2,1,0:T(8,128)S(1)} %copy-done.1, f32[3,16,16,128]{3,2,1,0:T(8,128)S(1)} %copy-done, f32[16,16,128]{2,1,0:T(8,128)S(1)} %copy-done.2, f32[128,2000]{1,0:T(8,128)S(1)} %copy.11.obs_far, ...), custom_call_target="tpu_custom_call" | custom-call | tf_op jit(solution)/shard_map/pallas_call | solution.py:433
  95.1 0.7 copy.17
  95.7 0.7 copy.18
  96.5 0.6 copy.19
Async XLA Ops:
  1.3 0.7 copy-start.5
  2.0 1.7 %copy-start = (f32[3,16,16,128]{3,2,1,0:T(8,128)S(1)}, f32[3,16,16,128]{3,2,1,0:T(8,128)}, u32[]{:S(2)}) copy-start(f32[3,16,16,128]{3,2,1,0:T(8,128)} %vel_ref.1) | copy-start | bytes 1179652
  2.1 1.7 %copy-start.1 = (f32[16,16,128]{2,1,0:T(8,128)S(1)}, f32[16,16,128]{2,1,0:T(8,128)}, u32[]{:S(2)}) copy-start(f32[16,16,128]{2,1,0:T(8,128)} %press_ref.1) | copy-start | bytes 393220
  2.1 1.7 %copy-start.2 = (f32[16,16,128]{2,1,0:T(8,128)S(1)}, f32[16,16,128]{2,1,0:T(8,128)}, u32[]{:S(2)}) copy-start(f32[16,16,128]{2,1,0:T(8,128)} %cour_ref.1) | copy-start | bytes 393220
  2.1 1.7 %copy-start.3 = (s32[128]{0:T(128)S(1)}, s32[128]{0:T(128)}, u32[]{:S(2)}) copy-start(s32[128]{0:T(128)} %param.13) | copy-start | bytes 1540
  2.1 1.7 %copy-start.4 = (f32[20]{0:T(128)S(1)}, f32[20]{0:T(128)}, u32[]{:S(2)}) copy-start(f32[20]{0:T(128)} %wave_ref.1) | copy-start | bytes 244

commit v3 on v2

--- a/solution.py
+++ b/solution.py
@@ -300,20 +300,37 @@
         grad_z = cour * slope(shifted_z(fz, 1), fz, shifted_z(fz, 2), shifted_z(fz, -1))
         return (grad_x, grad_y, grad_z, fz, cour)
 
-    def update(b, first, last, amplitude):
-        n = last - first
-        grad_x, grad_y, grad_z, total, cour = grads(b, first, last)
-        acc = slope(grad_x[2 : 2 + n], grad_x[1 : 1 + n], grad_x[3 : 3 + n], grad_x[0:n])
+    def early(b, first, last, amplitude):
+        fy = field[b, first + HALO : last + HALO]
+        grad_y = speed[first + HALO : last + HALO] * slope(
+            shifted(fy, 1, 1), fy, shifted(fy, 2, 1), shifted(fy, -1, 1)
+        )
+        fz = fy[:, SIDE : SIDE + cy]
+        cour = cour_ref[first:last]
+        grad_z = cour * slope(shifted_z(fz, 1), fz, shifted_z(fz, 2), shifted_z(fz, -1))
         acc_y = slope(
             grad_y, shifted(grad_y, -1, 1), shifted(grad_y, 1, 1), shifted(grad_y, -2, 1)
         )
-        acc = acc + acc_y[:, SIDE : SIDE + cy]
-        acc = acc + slope(
+        acc = acc_y[:, SIDE : SIDE + cy] + slope(
             grad_z, shifted_z(grad_z, -1), shifted_z(grad_z, 1), shifted_z(grad_z, -2)
         )
-        fresh = now[first:last] + (cour * acc - base[first:last]) + amplitude * mark[first:last]
+        now[first:last] = now[first:last] + (
+            (cour * acc - base[first:last]) + amplitude * mark[first:last]
+        )
+
+    def late(b, first, last):
+        n = last - first
+        m = n + 3
+        fx = field[b, first : last + 2 * HALO, SIDE : SIDE + cy, :]
+        grad_x = speed[first + 1 : last + 4, SIDE : SIDE + cy, :] * slope(
+            fx[2 : 2 + m], fx[1 : 1 + m], fx[3 : 3 + m], fx[0:m]
+        )
+        acc = slope(grad_x[2 : 2 + n], grad_x[1 : 1 + n], grad_x[3 : 3 + n], grad_x[0:n])
+        fresh = now[first:last] + cour_ref[first:last] * acc
         now[first:last] = fresh
-        field[1 - b, first + HALO : last + HALO, SIDE : SIDE + cy, :] = total + fresh
+        field[1 - b, first + HALO : last + HALO, SIDE : SIDE + cy, :] = (
+            fx[HALO : HALO + n] + fresh
+        )
 
     def listen():
         each(lambda k: swap(0, codes_out, codes_in, k).wait())
@@ -343,13 +360,15 @@
 
         to_side(b).wait()
         amplitude = wave_ref[t]
+        early(b, 0, HALO, amplitude)
+        early(b, cx - HALO, cx, amplitude)
 
         @pl.when(has_low)
         def _():
             to_low(b).wait_send()
             to_high(b).wait_recv()
 
-        update(b, 0, HALO, amplitude)
+        late(b, 0, HALO)
 
         @pl.when(has_low & more)
         def _():
@@ -360,13 +379,14 @@
             to_high(b).wait_send()
             to_low(b).wait_recv()
 
-        update(b, cx - HALO, cx, amplitude)
+        late(b, cx - HALO, cx)
 
         @pl.when(has_high & more)
         def _():
             to_high(1 - b).start()
 
-        update(b, HALO, cx - HALO, amplitude)
+        early(b, HALO, cx - HALO, amplitude)
+        late(b, HALO, cx - HALO)
 
         @pl.when(more)
         def _():

time: 97.2 us -> 93.5 us (0.962)
  Pallas kernels: 91.3 us -> 87.5 us
    pallas_call x1, Pallas kernels: 91.3 us -> 87.5 us  [body(): pl.pallas_call(functools.partial(kernel, count_x, count_y, cap), out_shap...]
where the time goes in v3:
time: 93.5 us; the launch traced here: 93.3 us
  Pallas kernels  87.5 us (94%)
  local copies, waits for them, and re-layouts  4.4 us (5%)
  between operations  1.38 us (1%)
    pallas_call x1, Pallas kernels, body(): pl.pallas_call(functools.partial(kernel, count_x, count_y, cap), out_shap...  87.5 us
    unnamed x17, local copies, waits for them, and re-layouts  4.4 us

profile of v3, /device:TPU:0, one launch (start us, length us, event | category | flops | bytes accessed | tf_op | source)
XLA Modules:
  0.0 93.3 jit_solution(8238513027187038499)
XLA Ops:
  1.3 0.0 copy-start.5
  1.3 0.6 copy-done.5
  1.9 0.1 copy.12.owner_ref
  2.0 0.0 copy-start
  2.1 0.0 copy-start.1
  2.1 0.0 copy-start.2
  2.1 0.0 copy-start.3
  2.1 0.0 copy-start.4
  2.1 1.6 %copy.11.obs_far = f32[128,2000]{1,0:T(8,128)S(1)} copy(f32[128,2000]{0,1:T(8,128)} %param.11) | data formatting | bytes 2048000 | tf_op args[3]
  3.7 0.0 copy-done
  3.7 0.0 copy-done.1
  3.7 0.0 copy-done.2
  3.7 0.0 copy-done.3
  3.8 0.0 copy-done.4
  3.8 87.5 %shard_map.103 = (f32[16,16,128]{2,1,0:T(8,128)S(1)}, f32[3,16,16,128]{3,2,1,0:T(8,128)S(1)}, f32[1,2048]{1,0:T(1,128)S(1)}) custom-call(f32[16,16,128]{2,1,0:T(8,128)S(1)} %copy-done.1, f32[3,16,16,128]{3,2,1,0:T(8,128)S(1)} %copy-done, f32[16,16,128]{2,1,0:T(8,128)S(1)} %copy-done.2, f32[128,2000]{1,0:T(8,128)S(1)} %copy.11.obs_far, ...), custom_call_target="tpu_custom_call" | custom-call | tf_op jit(solution)/shard_map/pallas_call | solution.py:453
  91.3 0.7 copy.17
  91.9 0.7 copy.18
  92.7 0.6 copy.19
Async XLA Ops:
  1.3 0.7 copy-start.5
  2.0 1.7 %copy-start = (f32[3,16,16,128]{3,2,1,0:T(8,128)S(1)}, f32[3,16,16,128]{3,2,1,0:T(8,128)}, u32[]{:S(2)}) copy-start(f32[3,16,16,128]{3,2,1,0:T(8,128)} %vel_ref.1) | copy-start | bytes 1179652
  2.1 1.7 %copy-start.1 = (f32[16,16,128]{2,1,0:T(8,128)S(1)}, f32[16,16,128]{2,1,0:T(8,128)}, u32[]{:S(2)}) copy-start(f32[16,16,128]{2,1,0:T(8,128)} %press_ref.1) | copy-start | bytes 393220
  2.1 1.7 %copy-start.2 = (f32[16,16,128]{2,1,0:T(8,128)S(1)}, f32[16,16,128]{2,1,0:T(8,128)}, u32[]{:S(2)}) copy-start(f32[16,16,128]{2,1,0:T(8,128)} %cour_ref.1) | copy-start | bytes 393220
  2.1 1.7 %copy-start.3 = (s32[128]{0:T(128)S(1)}, s32[128]{0:T(128)}, u32[]{:S(2)}) copy-start(s32[128]{0:T(128)} %param.13) | copy-start | bytes 1540
  2.1 1.7 %copy-start.4 = (f32[20]{0:T(128)S(1)}, f32[20]{0:T(128)}, u32[]{:S(2)}) copy-start(f32[20]{0:T(128)} %wave_ref.1) | copy-start | bytes 244
